TPU v7x, 32 devices: a whole 2x2x4 slice. The times are simulated.
32 devices in a mesh: det: 4 (over y, x), tm: 8 (over z, core).
Axes of the slice: x: 2, y: 2, z: 4, core: 2. Of those that a mesh axis runs over, the one named last changes fastest.
Arguments:
- tod: float32 [64, 32768], P('det', 'tm'), may hold values from -6 to 6
- pointing: int32 [64, 32768], P('det', 'tm'), may hold values from 0 to 1535
- noise_level: float32 [4, 64], P(None, 'det'), may hold values from 0.5 to 4
- modes: float32 [4, 64, 128], P(None, 'det'), may hold values from -2 to 2
Outputs:
- filtered: float32 [64, 32768], P('det', 'tm')
- binned: float32 [1536], P(('det', 'tm'))
All inputs are finite; a program needn't handle non-finite values.
Results may differ from a plain program's by a relative error of at most 0.00026.
Values sent between devices are 32-bit elements; how exact they have to be, the bound alone decides.
A program may use at most 64 MiB of HBM per device.

v0:
```python
import math

import jax
import jax.numpy as jnp
from jax import lax
from jax.sharding import PartitionSpec as P

FA = 128
FB = 256
TPIX = 48


HIGHEST = lax.Precision.HIGHEST


def rotation_table(size, total, sign):
    index = jnp.arange(size, dtype=jnp.int32)
    product = index[:, None] * index[None, :] % total
    angle = 2.0 * math.pi / total * product.astype(jnp.float32)
    return (jnp.cos(angle), sign * jnp.sin(angle))


def transform(real_in, imag_in, rows, cols, sign, real_out):
    length = rows * cols
    count = real_in.shape[0]
    first_cos, first_sin = rotation_table(rows, rows, sign)
    last_cos, last_sin = rotation_table(cols, cols, sign)
    grid_real = real_in.reshape(count, rows, cols)
    section_real = jnp.einsum("jm,rmq->rjq", first_cos, grid_real, precision=HIGHEST)
    section_imag = jnp.einsum("jm,rmq->rjq", first_sin, grid_real, precision=HIGHEST)
    if imag_in is not None:
        grid_imag = imag_in.reshape(count, rows, cols)
        section_real = section_real - jnp.einsum(
            "jm,rmq->rjq", first_sin, grid_imag, precision=HIGHEST
        )
        section_imag = section_imag + jnp.einsum(
            "jm,rmq->rjq", first_cos, grid_imag, precision=HIGHEST
        )
    row_index = jnp.arange(rows, dtype=jnp.int32)
    col_index = jnp.arange(cols, dtype=jnp.int32)
    turn = (row_index[:, None] * col_index[None, :] % length).astype(jnp.float32) * (
        2.0 * math.pi / length
    )
    turn_cos = jnp.cos(turn)
    turn_sin = sign * jnp.sin(turn)
    mixed_real = section_real * turn_cos - section_imag * turn_sin
    mixed_imag = section_real * turn_sin + section_imag * turn_cos
    out_real = jnp.einsum("km,rjm->rkj", last_cos, mixed_real, precision=HIGHEST) - jnp.einsum(
        "km,rjm->rkj", last_sin, mixed_imag, precision=HIGHEST
    )
    if real_out:
        return out_real.reshape(count, length)
    out_imag = jnp.einsum("km,rjm->rkj", last_sin, mixed_real, precision=HIGHEST) + jnp.einsum(
        "km,rjm->rkj", last_cos, mixed_imag, precision=HIGHEST
    )
    return (out_real.reshape(count, length), out_imag.reshape(count, length))


def solve_modes(factor, rhs):
    lower_part = lax.linalg.triangular_solve(factor, rhs, left_side=True, lower=True)
    return lax.linalg.triangular_solve(
        factor, lower_part, left_side=True, lower=True, transpose_a=True
    )


def band_of(freq, length, width, bands):
    folded = jnp.minimum(freq, length - freq)
    return jnp.minimum(folded // width, bands - 1)


def pick(array, index):
    return lax.dynamic_index_in_dim(array, index, 0, keepdims=False)


def body(tod, pointing, noise_level, modes):
    groups = lax.axis_size("tm")
    row_pos = lax.axis_index("tm")
    det_dev, block = tod.shape
    det_row = det_dev // groups
    length = block * groups
    bands = noise_level.shape[0]
    width = length // groups
    half_block = length // (2 * groups)
    mode_count = modes.shape[2]
    eye = jnp.eye(mode_count, dtype=jnp.float32)
    start = row_pos * half_block
    main_band = band_of(start, length, width, bands)
    side_band = jnp.int32(bands - 1)
    scaled = modes / noise_level[:, :, None]
    partial_all = jnp.einsum("bdm,bdn->bmn", modes, scaled, precision=HIGHEST)
    summed = lax.psum(partial_all, "det")
    gram_main = pick(summed, main_band) + eye
    gram_side = pick(summed, side_band) + eye
    factor_main = jnp.linalg.cholesky(gram_main)
    factor_side = jnp.linalg.cholesky(gram_side)
    arranged = tod.reshape(groups, det_row, block)
    spec_real, spec_imag = transform(
        lax.all_to_all(arranged, "tm", split_axis=0, concat_axis=2, tiled=True)[0],
        None,
        FA,
        FB,
        -1.0,
        False,
    )
    spec_real, spec_imag = (spec_real[None], spec_imag[None])
    spec_real = spec_real[0]
    spec_imag = spec_imag[0]
    basis_main = pick(modes, main_band)
    inverse_main = 1.0 / pick(noise_level, main_band)
    basis_side = pick(modes, side_band)
    inverse_side = 1.0 / pick(noise_level, side_band)
    half = length // 2
    row_noise = lax.dynamic_slice_in_dim(inverse_side, row_pos * det_row, det_row)
    row_basis = lax.dynamic_slice_in_dim(basis_side, row_pos * det_row, det_row, 0)
    top_weighted = spec_real[:, half] * row_noise
    top_proj = jnp.dot(
        top_weighted, row_basis, precision=HIGHEST, preferred_element_type=jnp.float32
    )
    top_proj = lax.psum(top_proj, ("det", "tm"))
    band_real, band_imag = (
        lax.all_to_all(spec_real[:, :half], "tm", split_axis=1, concat_axis=0, tiled=True),
        lax.all_to_all(spec_imag[:, :half], "tm", split_axis=1, concat_axis=0, tiled=True),
    )
    stacked = jnp.concatenate([band_real, band_imag], axis=1) * inverse_main[:, None]
    proj_main = jnp.dot(
        basis_main.T, stacked, precision=HIGHEST, preferred_element_type=jnp.float32
    )
    proj_main = lax.psum(proj_main, "det")
    coef_main = solve_modes(factor_main, proj_main)
    out_main = (
        stacked
        - jnp.dot(basis_main, coef_main, precision=HIGHEST, preferred_element_type=jnp.float32)
        * inverse_main[:, None]
    )
    top_coef = solve_modes(factor_side, top_proj[:, None])[:, 0]
    top_out = (
        top_weighted
        - jnp.dot(row_basis, top_coef, precision=HIGHEST, preferred_element_type=jnp.float32)
        * row_noise
    )
    rows_real, rows_imag = (
        lax.all_to_all(out_main[:, :half_block], "tm", split_axis=0, concat_axis=1, tiled=True),
        lax.all_to_all(out_main[:, half_block:], "tm", split_axis=0, concat_axis=1, tiled=True),
    )
    full_real = jnp.concatenate(
        [rows_real, top_out[:, None], jnp.flip(rows_real[:, 1:], axis=1)], axis=1
    )
    full_imag = jnp.concatenate(
        [rows_imag, jnp.zeros((det_row, 1), jnp.float32), -jnp.flip(rows_imag[:, 1:], axis=1)],
        axis=1,
    )
    filtered_rows = transform(full_real, full_imag, FB, FA, 1.0, True) * (1.0 / length)
    filtered = lax.all_to_all(filtered_rows, "tm", split_axis=1, concat_axis=0, tiled=True)
    pixels = TPIX * lax.axis_size("det") * groups
    flat_pointing = pointing.reshape(-1)
    sums = jax.ops.segment_sum(filtered.reshape(-1), flat_pointing, num_segments=pixels)
    hits = jax.ops.segment_sum(
        jnp.ones(flat_pointing.shape, jnp.float32), flat_pointing, num_segments=pixels
    )
    sums, hits = (
        lax.psum_scatter(sums, ("det", "tm"), scatter_dimension=0, tiled=True),
        lax.psum_scatter(hits, ("det", "tm"), scatter_dimension=0, tiled=True),
    )
    return (filtered, sums / jnp.sqrt(1.0 + hits))


def solution(mesh):
    placed = (P("det", "tm"), P("det", "tm"), P(None, "det"), P(None, "det", None))
    return jax.shard_map(
        body,
        mesh=mesh,
        in_specs=placed,
        out_specs=(P("det", "tm"), P(("det", "tm"))),
        check_vma=False,
    )
```

profile of v0, /device:TPU:0, one launch (start us, length us, event | category | flops | bytes accessed | tf_op | source)
XLA Modules:
  0.0 1193.3 jit_solution(8421175890699902363)
XLA Ops:
  7.2 1.8 reshape.144
  9.0 6.3 all-to-all-start
  16.6 8.4 all-to-all-done
  29.3 1.4 fusion.6
  31.7 3.4 all-to-all-start.1
  37.5 4.3 all-to-all-done.1
  41.8 3.4 all-to-all-start.2
  46.7 5.2 all-to-all-done.2
  52.0 3.2 fusion.49
  56.0 39.9 %psum.23 = f32[128]{0:T(128)S(1)} all-reduce(f32[128]{0:T(128)S(1)} %convolution_bitcast_fusion.4), channel_id=1, replica_groups=mesh['det'=4,'tm'=8] {'det','tm'}, use_global_device_ids=true, to_apply=%region_4.6 | all-reduce | flops 128 | bytes 1024 | tf_op jit(solution)/shard_map/psum | solution.py:119
  96.0 33.2 %all-reduce.6.cloned.1.call-done = (f32[128,4096]{1,0:T(8,128)}, f32[4,128,128]{1,2,0:T(8,128)}) async-done(((f32[128,4096]{1,0:T(8,128)}, f32[4,128,128]{1,2,0:T(8,128)}), (f32[128,4096]{1,0:T(8,128)}, f32[4,128,128]{1,2,0:T(8,128)})) %all-reduce.6.cloned.1.call-update) | async-done | bytes 2359312 | tf_op jit(solution)/shard_map/psum | solution.py:128
  130.2 11.7 cholesky.44
  143.3 9.8 custom-call.12
  153.1 3.5 fusion.90
  156.6 1.9 fusion.88
  160.3 4.9 all-to-all-start.4
  166.2 11.7 cholesky.55
  179.2 9.8 custom-call.13
  190.4 5.1 all-to-all-start.3
  195.7 6.6 all-to-all-done.3
  202.5 11.1 reverse
  213.9 1.5 dynamic-update-slice.7
  215.5 1.5 fusion.17
  216.9 1.5 fusion.15
  218.4 11.1 reverse.1
  230.1 1.5 dynamic-update-slice.4
  231.6 1.5 fusion.4
  233.1 1.5 fusion.3
  237.3 3.4 all-to-all-start.5
  240.8 451.9 %scatter_custom_fusion.1 = f32[1536]{0:T(1024)S(1)} fusion(s32[65536]{0:T(1024)S(1)} %bitcast.195, f32[65536]{0:T(1024)S(1)} %broadcast.244, f32[]{:T(128)} %constant.165.clone.1), kind=kCustom, calls=%fused_computation.151 | custom fusion | flops 65536 | bytes 6148 | tf_op jit(solution)/shard_map/scatter-add | solution.py:157
  692.8 451.9 %scatter_custom_fusion = f32[1536]{0:T(1024)S(1)} fusion(s32[65536]{0:T(1024)S(1)} %bitcast.196, f32[65536]{0:T(1024)S(1)} %bitcast.197, f32[]{:T(128)} %constant.165.clone.1), kind=kCustom, calls=%fused_computation.153 | custom fusion | flops 65536 | bytes 6148 | tf_op jit(solution)/shard_map/scatter-add | solution.py:156
  1145.6 39.8 %all-reduce.2 = (f32[1536]{0:T(1024)S(1)}, f32[1536]{0:T(1024)S(1)}) all-reduce(f32[1536]{0:T(1024)S(1)} %scatter_custom_fusion.1, f32[1536]{0:T(1024)S(1)} %scatter_custom_fusion), channel_id=3, replica_groups=mesh['det'=4,'tm'=8] {'det','tm'}, use_global_device_ids=true, to_apply=%region_8.10.clone | all-reduce | flops 3072 | bytes 24576
  (70 shorter events, 24.5 us)
Async XLA Ops:
  9.0 16.1 %all-to-all-start = ((f32[8,2,4096]{2,1,0:T(2,128)}), f32[8,2,4096]{2,1,0:T(2,128)S(1)}, u32[]{:S(2)}, u32[]{:S(2)}) async-start(f32[8,2,4096]{2,1,0:T(2,128)} %reshape.144), calls=%async_computation | async-start | bytes 524288 | tf_op jit(solution)/shard_map/all_to_all | solution.py:98
  30.8 14.4 %copy-start.1 = (f32[4,16,128]{2,1,0:T(8,128)S(1)}, f32[4,16,128]{2,1,0:T(8,128)}, u32[]{:S(2)}) copy-start(f32[4,16,128]{2,1,0:T(8,128)} %param.8) | copy-start | bytes 98308
  30.8 14.4 %copy-start.2 = (f32[4,16]{1,0:T(4,128)S(1)}, f32[4,16]{1,0:T(4,128)}, u32[]{:S(2)}) copy-start(f32[4,16]{1,0:T(4,128)} %param.7) | copy-start | bytes 772
  31.7 10.1 all-to-all-start.1
  41.8 10.1 all-to-all-start.2
  45.2 84.0 %all-reduce.6.cloned.1.call-start = ((), (), s32[]{:S(2)}) async-start(), calls=%async_computation.6 | async-start | bytes 4718592 | tf_op jit(solution)/shard_map/psum | solution.py:128
  160.3 30.1 %all-to-all-start.4 = ((f32[8,2,2048]{2,1,0:T(2,128)}), f32[8,2,2048]{2,1,0:T(2,128)S(1)}, u32[]{:S(2)}, u32[]{:S(2)}) async-start(f32[8,2,2048]{2,1,0:T(2,128)} %all_to_all.94), calls=%async_computation.4 | async-start | bytes 262144 | tf_op jit(solution)/shard_map/all_to_all | solution.py:143
  190.4 11.9 all-to-all-start.3
  234.6 6.1 copy-start
  237.3 455.5 %all-to-all-start.5 = ((f32[2,8,4096]{2,0,1:T(2,128)}), f32[2,8,4096]{2,0,1:T(2,128)S(1)}, u32[]{:S(2)}, u32[]{:S(2)}) async-start(f32[2,8,4096]{2,0,1:T(2,128)} %copy.60), calls=%async_computation.5 | async-start | bytes 524288 | tf_op jit(solution)/shard_map/all_to_all | solution.py:153
Sparse Core Ops, SparseCore 0:
  55.3 73.8 all-reduce.5
where the time goes:
time: 1200 us; the launch traced here: 1190 us
  other arithmetic  954 us (80%)
  blocking collectives  79.8 us (7%)
  waiting for transfers between devices  57.8 us (5%)
  local copies, waits for them, and re-layouts  34.4 us (3%)
  starting transfers between devices  26.5 us (2%)
  matrix products  26 us (2%)
  between operations  14.9 us (1%)
    scatter-add x1, other arithmetic, body(): jax.ops.segment_sum(jnp.ones(flat_pointing.shape, jnp.float32), flat_poin...  452 us
    scatter-add x1, other arithmetic, body(): jax.ops.segment_sum(filtered.reshape(-1), flat_pointing, num_segments=pix...  452 us
    psum x1, blocking collectives, body(): top_proj = lax.psum(top_proj, ('det', 'tm'))  39.9 us
    unnamed x1, blocking collectives  39.8 us
    psum x1, waiting for transfers between devices, body(): proj_main = lax.psum(proj_main, 'det')  33.2 us
  transfers between devices with their start and end apart: 7, of which 5 were waited for; matrix products, arithmetic and copies ran while one was open for 40% of the time, Pallas kernels for 0%

commit v1 on v0

--- a/solution.py
+++ b/solution.py
@@ -1,8 +1,12 @@
+import functools
 import math
 
 import jax
 import jax.numpy as jnp
+import numpy as np
 from jax import lax
+from jax.experimental import pallas as pl
+from jax.experimental.pallas import tpu as pltpu
 from jax.sharding import PartitionSpec as P
 
 FA = 128
@@ -72,7 +76,7 @@
     return lax.dynamic_index_in_dim(array, index, 0, keepdims=False)
 
 
-def body(tod, pointing, noise_level, modes):
+def general_body(tod, pointing, noise_level, modes):
     groups = lax.axis_size("tm")
     row_pos = lax.axis_index("tm")
     det_dev, block = tod.shape
@@ -164,6 +168,418 @@
     return (filtered, sums / jnp.sqrt(1.0 + hits))
 
 
+N1 = 128
+N2 = 256
+CHUNKS = 32
+MESH = pl.DeviceIdType.MESH
+NT = (((1,), (1,)), ((), ()))
+NN = (((1,), (0,)), ((), ()))
+
+
+def halves(table):
+    table = np.asarray(table, np.float32)
+    high = table.astype(jnp.bfloat16)
+    low = (table - high.astype(np.float32)).astype(jnp.bfloat16)
+    return np.stack([np.asarray(high), np.asarray(low)])
+
+
+def tables():
+    length = N1 * N2
+    half = N1 // 2
+    n1 = np.arange(N1)
+    n2 = np.arange(N2)
+    k1 = np.arange(half)
+    angle = 2 * np.pi * (k1[:, None] * n1[None, :] % N1) / N1
+    first = np.concatenate([np.cos(angle), -np.sin(angle)])
+    first[half] = np.cos(np.pi * n1)
+    turn = 2 * np.pi * (k1[:, None] * n2[None, :]) / length
+    tc, ts = np.cos(turn), np.sin(turn)
+    t1 = np.concatenate([tc, tc])
+    t2 = np.concatenate([ts, -ts])
+    t3 = np.concatenate([-ts, -ts])
+    t4 = np.concatenate([tc, -tc])
+    t1[0], t2[0], t3[0], t4[0] = 1.0, 0.0, 1.0, 0.0
+    b = np.pi * n2 / N2
+    t1[half], t2[half] = np.cos(b) + np.sin(b), 0.0
+    t3[half], t4[half] = np.cos(b) - np.sin(b), 0.0
+    twiddle = np.stack([t1, t2, t3, t4]).astype(np.float32)
+    angle = 2 * np.pi * (n2[:, None] * n2[None, :] % N2) / N2
+    last = np.concatenate([np.cos(angle), np.sin(angle)], axis=1)
+    weight = np.full((N1,), 2.0 / length)
+    weight[0] = weight[half] = 1.0 / length
+    return (
+        halves(first),
+        twiddle,
+        halves(last),
+        halves(last.T),
+        np.ascontiguousarray(np.swapaxes(twiddle, 1, 2)),
+        halves(first.T * weight[None, :]),
+    )
+
+
+def split(x):
+    high = x.astype(jnp.bfloat16)
+    return high, (x - high.astype(jnp.float32)).astype(jnp.bfloat16)
+
+
+def dot(a, b, dims):
+    return lax.dot_general(a, b, dims, preferred_element_type=jnp.float32)
+
+
+def dot3(a, b, dims):
+    return dot(a[0], b[0], dims) + dot(a[0], b[1], dims) + dot(a[1], b[0], dims)
+
+
+def invert_pair(matrix):
+    size, lanes = matrix.shape
+    row = lax.broadcasted_iota(jnp.int32, (size, lanes), 0)
+    lane = lax.broadcasted_iota(jnp.int32, (size, lanes), 1)
+    left = lane < size
+    column = jnp.where(left, lane, lane - size)
+
+    def step(k, a):
+        at_row = row == k
+        at_col = column == k
+        picked = jnp.where(at_col, a, 0.0)
+        one = jnp.sum(jnp.where(left, picked, 0.0), axis=1, keepdims=True)
+        two = jnp.sum(jnp.where(left, 0.0, picked), axis=1, keepdims=True)
+        c = jnp.where(left, one, two)
+        pivot = jnp.sum(jnp.where(at_row, c, 0.0), axis=0, keepdims=True)
+        r = jnp.sum(jnp.where(at_row, jnp.where(at_col, 1.0, a), 0.0), axis=0, keepdims=True)
+        r = r * (1.0 / pivot)
+        base = jnp.where(at_row | at_col, 0.0, a)
+        return base - jnp.where(at_row, -1.0, c) * r
+
+    return lax.fori_loop(0, size, step, matrix)
+
+
+def expand(matrix):
+    size = matrix.shape[0]
+    big = size * 8
+    spread = (
+        lax.broadcasted_iota(jnp.int32, (big, size), 0) // 8
+        == lax.broadcasted_iota(jnp.int32, (big, size), 1)
+    )
+    spread = jnp.where(spread, 1.0, 0.0).astype(jnp.bfloat16)
+    same = (
+        lax.broadcasted_iota(jnp.int32, (big, big), 0) % 8
+        == lax.broadcasted_iota(jnp.int32, (big, big), 1) % 8
+    )
+    out = []
+    for part in split(matrix):
+        tall = dot(spread, part, NN).astype(jnp.bfloat16)
+        wide = dot(tall, spread, NT)
+        out.append(jnp.where(same, wide, 0.0).astype(jnp.bfloat16))
+    return out
+
+
+def fused(
+    groups,
+    dets,
+    tod_ref,
+    owner_ref,
+    inside_ref,
+    mode_ref,
+    noise_ref,
+    first_ref,
+    twiddle_ref,
+    last_ref,
+    last_t_ref,
+    twiddle_t_ref,
+    first_t_ref,
+    out_ref,
+    map_ref,
+    x_in,
+    modes_all,
+    noise_all,
+    spec_send,
+    spec_recv,
+    back_send,
+    back_recv,
+    time_send,
+    kron,
+    map_send,
+    map_recv,
+    mode_sems,
+    noise_sems,
+    tod_sems,
+    spec_sems,
+    back_sems,
+    time_sems,
+    map_sems,
+):
+    i = lax.axis_index("det")
+    t = lax.axis_index("tm")
+    total = groups * dets
+    me = i * groups + t
+    chunk = t * dets + i
+    per = mode_ref.shape[1]
+
+    def place(p):
+        q = p // groups
+        return q, p - q * groups
+
+    barrier = pltpu.get_barrier_semaphore()
+
+    def greet(j, carry):
+        q, u = place(lax.rem(me + j, total))
+        pl.semaphore_signal(barrier, inc=1, device_id=(q, u), device_id_type=MESH)
+        return carry
+
+    lax.fori_loop(1, total, greet, 0)
+    pl.semaphore_wait(barrier, total - 1)
+
+    def remote(src, dst, sems, j, where):
+        return pltpu.make_async_remote_copy(
+            src_ref=src,
+            dst_ref=dst,
+            send_sem=sems.at[0, j],
+            recv_sem=sems.at[1, j],
+            device_id=where,
+            device_id_type=MESH,
+        )
+
+    def mode_copy(j):
+        rows = pl.ds(pl.multiple_of(i * per, per), per)
+        return remote(
+            mode_ref, modes_all.at[:, rows, :], mode_sems, j, (lax.rem(i + j, dets), t)
+        )
+
+    def noise_copy(j):
+        rows = pl.ds(pl.multiple_of(i * per, per), per)
+        return remote(
+            noise_ref, noise_all.at[:, rows, :], noise_sems, j, (lax.rem(i + j, dets), t)
+        )
+
+    def tod_copy(j):
+        u = lax.rem(t + j, groups)
+        rows = pl.ds(pl.multiple_of(t * 16, 16), 16)
+        return remote(tod_ref.at[u], x_in.at[:, rows, :], tod_sems, j, (i, u))
+
+    def spec_copy(j):
+        q, u = place(lax.rem(me + j, total))
+        return remote(spec_send.at[u * dets + q], spec_recv.at[me], spec_sems, j, (q, u))
+
+    def back_copy(j):
+        p = lax.rem(me + j, total)
+        return remote(back_send.at[p], back_recv.at[chunk], back_sems, j, place(p))
+
+    def time_copy(j):
+        u = lax.rem(t + j, groups)
+        rows = pl.ds(pl.multiple_of(u * 16, 16), 16)
+        return remote(time_send.at[:, rows, :], out_ref.at[t], time_sems, j, (i, u))
+
+    def map_copy(j):
+        p = lax.rem(me + j, total)
+        return remote(map_send.at[p], map_recv.at[me], map_sems, j, place(p))
+
+    def start_all(make, count):
+        def go(j, carry):
+            make(j).start()
+            return carry
+
+        lax.fori_loop(1, count, go, 0)
+
+    def wait_all(make, count):
+        def go(j, carry):
+            make(j).wait()
+            return carry
+
+        lax.fori_loop(1, count, go, 0)
+
+    start_all(mode_copy, dets)
+    start_all(noise_copy, dets)
+    start_all(tod_copy, groups)
+
+    own_rows = pl.ds(pl.multiple_of(i * per, per), per)
+    modes_all[:, own_rows, :] = mode_ref[...]
+    noise_all[:, own_rows, :] = noise_ref[...]
+    x_in[:, pl.ds(pl.multiple_of(t * 16, 16), 16), :] = tod_ref[t]
+    wait_all(mode_copy, dets)
+    wait_all(noise_copy, dets)
+
+    count = modes_all.shape[1]
+    square = (count, count)
+    diagonal = lax.broadcasted_iota(jnp.int32, square, 0) == lax.broadcasted_iota(
+        jnp.int32, square, 1
+    )
+    sides = []
+    for s in range(2):
+        basis = modes_all[s]
+        outer = lax.dot_general(
+            basis, basis, NT, precision=HIGHEST, preferred_element_type=jnp.float32
+        )
+        sides.append(outer + jnp.where(diagonal, noise_all[s][:, :count], 0.0))
+    inverse = invert_pair(jnp.concatenate(sides, axis=1))
+    for s in range(2):
+        parts = expand(inverse[:, s * count : (s + 1) * count])
+        kron[s, 0] = parts[0]
+        kron[s, 1] = parts[1]
+
+    wait_all(tod_copy, groups)
+    grid = jnp.concatenate([x_in[0], x_in[1]], axis=1)
+    section = dot3((first_ref[0], first_ref[1]), split(grid), NN)
+    swapped = jnp.concatenate([section[N1 // 2 :], section[: N1 // 2]], axis=0)
+    rows = []
+    for d in range(2):
+        part = section[:, d * N2 : (d + 1) * N2]
+        other = swapped[:, d * N2 : (d + 1) * N2]
+        rows.append(
+            jnp.concatenate(
+                [
+                    part * twiddle_ref[0] + other * twiddle_ref[1],
+                    part * twiddle_ref[2] + other * twiddle_ref[3],
+                ],
+                axis=1,
+            )
+        )
+    spectrum = dot3((last_ref[0], last_ref[1]), split(jnp.concatenate(rows, axis=0)), NT)
+    for d in range(2):
+        spec_send[:, d * 8 : (d + 1) * 8, :] = spectrum[:, d * N1 : (d + 1) * N1].reshape(
+            CHUNKS, 8, N1
+        )
+    start_all(spec_copy, total)
+    spec_recv[me] = spec_send[chunk]
+    wait_all(spec_copy, total)
+
+    data = split(spec_recv[...].reshape(total * 16, N1))
+    main = dot3((kron[0, 0], kron[0, 1]), data, NN)
+    side = dot3((kron[1, 0], kron[1, 1]), data, NN)
+    shape = (total * 16, N1)
+    edge = (lax.broadcasted_iota(jnp.int32, shape, 0) % 8 == 0) & (
+        lax.broadcasted_iota(jnp.int32, shape, 1) == 0
+    )
+    apart = jnp.where((t > groups // 2) & (i == 0), 1, 0)
+    edge = edge & (jnp.full(shape, apart, jnp.int32) == 1)
+    back_send[...] = jnp.where(edge, side, main).reshape(total, 16, N1)
+    start_all(back_copy, total)
+    back_recv[chunk] = back_send[me]
+    wait_all(back_copy, total)
+
+    weighted = jnp.concatenate(
+        [back_recv[:, d * 8 : (d + 1) * 8, :].reshape(N2, N1) for d in range(2)], axis=1
+    )
+    spread = dot3((last_t_ref[0], last_t_ref[1]), split(weighted), NN)
+    upright = []
+    for d in range(2):
+        p = spread[:N2, d * N1 : (d + 1) * N1]
+        q = spread[N2:, d * N1 : (d + 1) * N1]
+        crossed = p * twiddle_t_ref[1] + q * twiddle_t_ref[3]
+        upright.append(
+            p * twiddle_t_ref[0]
+            + q * twiddle_t_ref[2]
+            + jnp.concatenate([crossed[:, N1 // 2 :], crossed[:, : N1 // 2]], axis=1)
+        )
+    stamped = dot3(
+        (first_t_ref[0], first_t_ref[1]), split(jnp.concatenate(upright, axis=0)), NT
+    )
+    for d in range(2):
+        time_send[d] = stamped[:, d * N2 : (d + 1) * N2]
+    start_all(time_copy, groups)
+    out_ref[t] = time_send[:, pl.ds(pl.multiple_of(t * 16, 16), 16), :]
+    wait_all(time_copy, groups)
+
+    width = 8 * N2
+    own_index = lax.broadcasted_iota(jnp.int32, (total, width), 0)
+    inside_index = lax.broadcasted_iota(jnp.int32, (TPIX, width), 0)
+
+    def flat(block):
+        return jnp.concatenate([block[r : r + 1] for r in range(8)], axis=1)
+
+    def bin_rows(g, acc):
+        a = g // 4
+        b = g - a * 4
+        c = b // 2
+        rows = pl.ds(pl.multiple_of((b - c * 2) * 8, 8), 8)
+        high, low = split(flat(out_ref[a, c, rows, :]))
+        mine = jnp.broadcast_to(flat(owner_ref[a, c, rows, :]), (total, width)) == own_index
+        spot = jnp.broadcast_to(flat(inside_ref[a, c, rows, :]), (TPIX, width)) == inside_index
+        high = jnp.where(mine, jnp.broadcast_to(high.astype(jnp.float32), (total, width)), 0.0)
+        low = jnp.where(mine, jnp.broadcast_to(low.astype(jnp.float32), (total, width)), 0.0)
+        ones = jnp.where(mine, 1.0, 0.0)
+        lhs = jnp.concatenate([high, low, ones], axis=0).astype(jnp.bfloat16)
+        rhs = jnp.where(spot, 1.0, 0.0).astype(jnp.bfloat16)
+        return acc + dot(lhs, rhs, NT)
+
+    acc = lax.fori_loop(0, 4 * groups, bin_rows, jnp.zeros((3 * total, TPIX), jnp.float32))
+    acc = jnp.concatenate([acc, jnp.zeros((3 * total, 128 - TPIX), jnp.float32)], axis=1)
+    map_send[...] = jnp.zeros(map_send.shape, jnp.float32)
+    map_send[:, 0, :] = acc[:total] + acc[total : 2 * total]
+    map_send[:, 1, :] = acc[2 * total :]
+    start_all(map_copy, total)
+    map_recv[me] = map_send[me]
+    wait_all(map_copy, total)
+    summed = jnp.sum(map_recv[...], axis=0)
+    map_ref[...] = jnp.broadcast_to(summed[0:1] / jnp.sqrt(1.0 + summed[1:2]), map_ref.shape)
+
+
+def fast_body(tod, pointing, noise_level, modes):
+    groups = lax.axis_size("tm")
+    dets = lax.axis_size("det")
+    t = lax.axis_index("tm")
+    det_dev = tod.shape[0]
+    bands = noise_level.shape[0]
+    total = groups * dets
+    main_band = jnp.minimum(t, groups - 1 - t)
+    side_band = jnp.minimum(main_band + 1, bands - 1)
+    blocks = (groups, det_dev // groups, 16, N2)
+    owner = (pointing // TPIX).reshape(blocks)
+    inside = (pointing % TPIX).reshape(blocks)
+    pair_modes = jnp.stack([pick(modes, main_band), pick(modes, side_band)])
+    pair_noise = jnp.stack([pick(noise_level, main_band), pick(noise_level, side_band)])
+    pair_noise = jnp.broadcast_to(pair_noise[:, :, None], pair_modes.shape)
+    everyone = det_dev * dets
+    f32 = jnp.float32
+    constants = [jnp.asarray(c) for c in tables()]
+    vmem = pl.BlockSpec(memory_space=pltpu.VMEM)
+    out, binned = pl.pallas_call(
+        functools.partial(fused, groups, dets),
+        out_shape=(
+            jax.ShapeDtypeStruct(blocks, f32),
+            jax.ShapeDtypeStruct((8, 128), f32),
+        ),
+        in_specs=[vmem] * (5 + len(constants)),
+        out_specs=(vmem, vmem),
+        scratch_shapes=[
+            pltpu.VMEM((2, N1, N2), f32),
+            pltpu.VMEM((2, everyone, 128), f32),
+            pltpu.VMEM((2, everyone, 128), f32),
+            pltpu.VMEM((total, 16, 128), f32),
+            pltpu.VMEM((total, 16, 128), f32),
+            pltpu.VMEM((total, 16, 128), f32),
+            pltpu.VMEM((total, 16, 128), f32),
+            pltpu.VMEM((2, N1, N2), f32),
+            pltpu.VMEM((2, 2, everyone * 8, everyone * 8), jnp.bfloat16),
+            pltpu.VMEM((total, 8, 128), f32),
+            pltpu.VMEM((total, 8, 128), f32),
+            pltpu.SemaphoreType.DMA((2, dets)),
+            pltpu.SemaphoreType.DMA((2, dets)),
+            pltpu.SemaphoreType.DMA((2, groups)),
+            pltpu.SemaphoreType.DMA((2, total)),
+            pltpu.SemaphoreType.DMA((2, total)),
+            pltpu.SemaphoreType.DMA((2, groups)),
+            pltpu.SemaphoreType.DMA((2, total)),
+        ],
+        compiler_params=pltpu.CompilerParams(
+            collective_id=0, has_side_effects=True, vmem_limit_bytes=40 * 1024 * 1024
+        ),
+    )(tod.reshape(blocks), owner, inside, pair_modes, pair_noise, *constants)
+    return out.reshape(tod.shape), binned[0, :TPIX]
+
+
+def body(tod, pointing, noise_level, modes):
+    groups = lax.axis_size("tm")
+    dets = lax.axis_size("det")
+    fits = (
+        groups * dets == CHUNKS
+        and groups == 2 * noise_level.shape[0]
+        and tod.shape == (2 * groups, N1 * N2 // groups)
+        and modes.shape[2] == 128
+        and 16 * groups == N1
+    )
+    return (fast_body if fits else general_body)(tod, pointing, noise_level, modes)
+
+
 def solution(mesh):
     placed = (P("det", "tm"), P("det", "tm"), P(None, "det"), P(None, "det", None))
     return jax.shard_map(

time: 1200 us -> 67.2 us (0.06)
  other arithmetic: 954 us -> 0.27 us
  blocking collectives: 79.8 us -> 0 us
  Pallas kernels: 0 us -> 60.8 us
  waiting for transfers between devices: 57.8 us -> 0 us
  local copies, waits for them, and re-layouts: 34.4 us -> 5.15 us
  starting transfers between devices: 26.5 us -> 0 us
  matrix products: 26 us -> 0 us
  between operations: 14.9 us -> 0.75 us
    scatter-add x2 -> x0, other arithmetic: 904 us -> none  [the longest x1 452 us: body(): jax.ops.segment_sum(jnp.ones(flat_pointing.shape, jnp.float32), flat_poin...]
    pallas_call x0 -> x1, Pallas kernels: none -> 60.8 us  [fast_body(): pl.pallas_call(functools.partial(fused, groups, dets), out_shape=(jax.Sha...]
    another operation x10 -> x2, other arithmetic: 45.7 us -> 0.02 us  [the longest x1 0.01 us: fast_body(): jnp.stack([pick(noise_level, main_band), pick(noise_level, side_band)])]
    psum x1 -> x0, blocking collectives: 39.9 us -> none  [body(): top_proj = lax.psum(top_proj, ('det', 'tm'))]
    unnamed x1 -> x0, blocking collectives: 39.8 us -> none
    psum x1 -> x0, waiting for transfers between devices: 33.2 us -> none  [body(): proj_main = lax.psum(proj_main, 'det')]
    all_to_all x6 -> x0, starting transfers between devices: 26.5 us -> none  [the longest x1 6.33 us: body(): lax.all_to_all(arranged, 'tm', split_axis=0, concat_axis=2, tiled=True)[0]]
    all_to_all x6 -> x0, waiting for transfers between devices: 24.5 us -> none  [the longest x1 8.44 us: body(): lax.all_to_all(arranged, 'tm', split_axis=0, concat_axis=2, tiled=True)[0]]
  transfers between devices with their start and end apart: 7 -> 0, of which waited for: 5 -> 0; matrix products, arithmetic and copies ran while one was open for 40% -> 0% of each run, Pallas kernels for 0% -> 0%
where the time goes in v1:
time: 67.2 us; the launch traced here: 67 us
  Pallas kernels  60.8 us (90%)
  local copies, waits for them, and re-layouts  5.15 us (8%)
  between operations  0.75 us (1%)
    pallas_call x1, Pallas kernels, fast_body(): pl.pallas_call(functools.partial(fused, groups, dets), out_shape=(jax.Sha...  60.8 us
    unnamed x20, local copies, waits for them, and re-layouts  3.84 us

profile of v1, /device:TPU:0, one launch (start us, length us, event | category | flops | bytes accessed | tf_op | source)
XLA Modules:
  0.0 67.0 jit_solution(426182808180938397)
XLA Ops:
  0.6 0.0 copy-start.7
  0.6 0.0 copy-start.6
  0.7 0.7 copy-done.7
  1.3 0.1 broadcast_in_dim.2.noise_ref
  1.4 0.7 %constant_dynamic-slice_fusion.3 = (f32[1,16,128]{2,1,0:T(8,128)S(1)}, f32[1,16,128]{2,1,0:T(8,128)S(1)}) fusion(f32[4,16,128]{2,1,0:T(8,128)} %param.13, s32[]{:T(128)S(6)} %select_n.24, s32[]{:T(128)S(6)} %select_n.25), kind=kLoop, calls=%fused_computation.10 | loop fusion | bytes 32776 | tf_op jit(solution)/shard_map/jit(dynamic_index_in_dim)/dynamic_slice | solution.py:76
  2.1 0.0 copy-start.3
  2.1 1.1 %copy.12 = f32[2,8,16,256]{3,2,1,0:T(8,128)S(1)} copy(f32[2,8,16,256]{3,1,2,0:T(8,128)} %bitcast.20) | data formatting | bytes 524288
  3.2 0.0 copy-done.6
  3.2 0.0 copy-start.2
  3.2 0.0 copy-start.4
  3.3 0.0 copy-start.5
  3.3 0.3 add_select_fusion
  3.5 0.0 copy-start
  3.5 0.0 copy-start.1
  3.6 0.1 copy.14
  3.6 0.1 copy.13
  3.7 0.0 copy-done.3
  3.7 0.5 copy-done.2
  4.3 0.0 copy-done.4
  4.3 0.0 copy-done.5
  4.3 0.3 copy-done
  4.6 0.2 copy-done.1
  4.8 60.8 %shard_map.113 = (f32[8,2,16,256]{3,2,1,0:T(8,128)S(1)}, f32[8,128]{1,0:T(8,128)S(1)}) custom-call(f32[8,2,16,256]{3,2,1,0:T(8,128)S(1)} %bitcast.14, s32[8,2,16,256]{3,2,1,0:T(8,128)S(1)} %bitcast.16, s32[8,2,16,256]{3,2,1,0:T(8,128)S(1)} %bitcast.15, f32[2,16,128]{2,1,0:T(8,128)S(1)} %pad_maximum_fusion.mode_ref, ...), custom_call_target="tpu_custom_call" | custom-call | tf_op jit(solution)/shard_map/pallas_call | solution.py:535
  65.6 0.9 %copy.15 = f32[2,8,16,256]{3,1,2,0:T(8,128)} copy(f32[2,8,16,256]{3,2,1,0:T(8,128)S(1)} %bitcast.17) | data formatting | bytes 524288
  66.5 0.5 slice_bitcast_fusion
  (3 shorter events, 0.0 us)
Async XLA Ops:
  0.6 0.7 %copy-start.7 = (f32[4,16]{1,0:T(4,128)S(1)}, f32[4,16]{1,0:T(4,128)}, u32[]{:S(2)}) copy-start(f32[4,16]{1,0:T(4,128)} %param.12) | copy-start | bytes 772
  0.6 2.6 %copy-start.6 = (s32[16,4096]{1,0:T(8,128)S(1)}, s32[16,4096]{1,0:T(8,128)}, u32[]{:S(2)}) copy-start(s32[16,4096]{1,0:T(8,128)} %param.11) | copy-start | bytes 786436
  2.1 1.6 %copy-start.3 = (f32[4,128,256]{2,1,0:T(8,128)S(1)}, f32[4,128,256]{2,1,0:T(8,128)}, u32[]{:S(2)}) copy-start(f32[4,128,256]{2,1,0:T(8,128)} %constant.55.clone.twiddle_ref) | copy-start | bytes 1572868
  3.2 1.0 %copy-start.2 = (bf16[2,256,512]{2,1,0:T(8,128)(2,1)S(1)}, bf16[2,256,512]{2,1,0:T(8,128)(2,1)}, u32[]{:S(2)}) copy-start(bf16[2,256,512]{2,1,0:T(8,128)(2,1)} %constant.56.clone.last_ref) | copy-start | bytes 1572868
  3.2 1.0 %copy-start.4 = (bf16[2,128,128]{2,1,0:T(8,128)(2,1)S(1)}, bf16[2,128,128]{2,1,0:T(8,128)(2,1)}, u32[]{:S(2)}) copy-start(bf16[2,128,128]{2,1,0:T(8,128)(2,1)} %constant.59.clone.first_t_ref) | copy-start | bytes 196612
  3.3 1.0 %copy-start.5 = (bf16[2,128,128]{2,1,0:T(8,128)(2,1)S(1)}, bf16[2,128,128]{2,1,0:T(8,128)(2,1)}, u32[]{:S(2)}) copy-start(bf16[2,128,128]{2,1,0:T(8,128)(2,1)} %constant.54.clone.first_ref) | copy-start | bytes 196612
  3.5 1.1 %copy-start = (f32[4,256,128]{2,1,0:T(8,128)S(1)}, f32[4,256,128]{2,1,0:T(8,128)}, u32[]{:S(2)}) copy-start(f32[4,256,128]{2,1,0:T(8,128)} %constant.58.clone.twiddle_t_ref) | copy-start | bytes 1572868
  3.5 1.2 %copy-start.1 = (bf16[2,512,256]{2,1,0:T(8,128)(2,1)S(1)}, bf16[2,512,256]{2,1,0:T(8,128)(2,1)}, u32[]{:S(2)}) copy-start(bf16[2,512,256]{2,1,0:T(8,128)(2,1)} %constant.57.clone.last_t_ref) | copy-start | bytes 1572868

commit v2 on v1

--- a/solution.py
+++ b/solution.py
@@ -171,6 +171,7 @@
 N1 = 128
 N2 = 256
 CHUNKS = 32
+UNROLL = 1
 MESH = pl.DeviceIdType.MESH
 NT = (((1,), (1,)), ((), ()))
 NN = (((1,), (0,)), ((), ()))
@@ -280,18 +281,16 @@
     owner_ref,
     inside_ref,
     mode_ref,
-    noise_ref,
-    first_ref,
-    twiddle_ref,
-    last_ref,
-    last_t_ref,
-    twiddle_t_ref,
-    first_t_ref,
+    first_hbm,
+    twiddle_hbm,
+    last_hbm,
+    last_t_hbm,
+    twiddle_t_hbm,
+    first_t_hbm,
     out_ref,
     map_ref,
     x_in,
     modes_all,
-    noise_all,
     spec_send,
     spec_recv,
     back_send,
@@ -300,8 +299,16 @@
     kron,
     map_send,
     map_recv,
+    first_ref,
+    twiddle_ref,
+    last_ref,
+    last_t_ref,
+    twiddle_t_ref,
+    first_t_ref,
+    masks,
+    spots,
+    load_sems,
     mode_sems,
-    noise_sems,
     tod_sems,
     spec_sems,
     back_sems,
@@ -315,6 +322,20 @@
     chunk = t * dets + i
     per = mode_ref.shape[1]
 
+    loads = [
+        pltpu.make_async_copy(src, dst, load_sems.at[n])
+        for n, (src, dst) in enumerate(
+            [
+                (first_hbm, first_ref),
+                (twiddle_hbm, twiddle_ref),
+                (last_hbm, last_ref),
+                (last_t_hbm, last_t_ref),
+                (twiddle_t_hbm, twiddle_t_ref),
+                (first_t_hbm, first_t_ref),
+            ]
+        )
+    ]
+
     def place(p):
         q = p // groups
         return q, p - q * groups
@@ -326,7 +347,9 @@
         pl.semaphore_signal(barrier, inc=1, device_id=(q, u), device_id_type=MESH)
         return carry
 
-    lax.fori_loop(1, total, greet, 0)
+    lax.fori_loop(1, total, greet, 0, unroll=UNROLL)
+    for load in loads:
+        load.start()
     pl.semaphore_wait(barrier, total - 1)
 
     def remote(src, dst, sems, j, where):
@@ -345,12 +368,6 @@
             mode_ref, modes_all.at[:, rows, :], mode_sems, j, (lax.rem(i + j, dets), t)
         )
 
-    def noise_copy(j):
-        rows = pl.ds(pl.multiple_of(i * per, per), per)
-        return remote(
-            noise_ref, noise_all.at[:, rows, :], noise_sems, j, (lax.rem(i + j, dets), t)
-        )
-
     def tod_copy(j):
         u = lax.rem(t + j, groups)
         rows = pl.ds(pl.multiple_of(t * 16, 16), 16)
@@ -378,44 +395,23 @@
             make(j).start()
             return carry
 
-        lax.fori_loop(1, count, go, 0)
+        lax.fori_loop(1, count, go, 0, unroll=UNROLL)
 
     def wait_all(make, count):
         def go(j, carry):
             make(j).wait()
             return carry
 
-        lax.fori_loop(1, count, go, 0)
+        lax.fori_loop(1, count, go, 0, unroll=UNROLL)
 
     start_all(mode_copy, dets)
-    start_all(noise_copy, dets)
     start_all(tod_copy, groups)
 
     own_rows = pl.ds(pl.multiple_of(i * per, per), per)
     modes_all[:, own_rows, :] = mode_ref[...]
-    noise_all[:, own_rows, :] = noise_ref[...]
     x_in[:, pl.ds(pl.multiple_of(t * 16, 16), 16), :] = tod_ref[t]
-    wait_all(mode_copy, dets)
-    wait_all(noise_copy, dets)
-
-    count = modes_all.shape[1]
-    square = (count, count)
-    diagonal = lax.broadcasted_iota(jnp.int32, square, 0) == lax.broadcasted_iota(
-        jnp.int32, square, 1
-    )
-    sides = []
-    for s in range(2):
-        basis = modes_all[s]
-        outer = lax.dot_general(
-            basis, basis, NT, precision=HIGHEST, preferred_element_type=jnp.float32
-        )
-        sides.append(outer + jnp.where(diagonal, noise_all[s][:, :count], 0.0))
-    inverse = invert_pair(jnp.concatenate(sides, axis=1))
-    for s in range(2):
-        parts = expand(inverse[:, s * count : (s + 1) * count])
-        kron[s, 0] = parts[0]
-        kron[s, 1] = parts[1]
-
+    for load in loads:
+        load.wait()
     wait_all(tod_copy, groups)
     grid = jnp.concatenate([x_in[0], x_in[1]], axis=1)
     section = dot3((first_ref[0], first_ref[1]), split(grid), NN)
@@ -440,6 +436,26 @@
         )
     start_all(spec_copy, total)
     spec_recv[me] = spec_send[chunk]
+    wait_all(mode_copy, dets)
+
+    count = modes_all.shape[1]
+    square = (count, count)
+    diagonal = lax.broadcasted_iota(jnp.int32, square, 0) == lax.broadcasted_iota(
+        jnp.int32, square, 1
+    )
+    sides = []
+    for s in range(2):
+        basis = modes_all[s, :, :128]
+        outer = lax.dot_general(
+            basis, basis, NT, precision=HIGHEST, preferred_element_type=jnp.float32
+        )
+        sides.append(outer + jnp.where(diagonal, modes_all[s, :, 128 : 128 + count], 0.0))
+    inverse = invert_pair(jnp.concatenate(sides, axis=1))
+    for s in range(2):
+        parts = expand(inverse[:, s * count : (s + 1) * count])
+        kron[s, 0] = parts[0]
+        kron[s, 1] = parts[1]
+
     wait_all(spec_copy, total)
 
     data = split(spec_recv[...].reshape(total * 16, N1))
@@ -454,6 +470,28 @@
     back_send[...] = jnp.where(edge, side, main).reshape(total, 16, N1)
     start_all(back_copy, total)
     back_recv[chunk] = back_send[me]
+
+    width = 8 * N2
+    own_index = lax.broadcasted_iota(jnp.int32, (total, width), 0)
+    inside_index = lax.broadcasted_iota(jnp.int32, (TPIX, width), 0)
+
+    def flat(block):
+        return jnp.concatenate([block[r : r + 1] for r in range(8)], axis=1)
+
+    def mark(g, acc):
+        a = g // 4
+        b = g - a * 4
+        c = b // 2
+        rows = pl.ds(pl.multiple_of((b - c * 2) * 8, 8), 8)
+        mine = jnp.broadcast_to(flat(owner_ref[a, c, rows, :]), (total, width)) == own_index
+        spot = jnp.broadcast_to(flat(inside_ref[a, c, rows, :]), (TPIX, width)) == inside_index
+        mine = jnp.where(mine, 1.0, 0.0).astype(jnp.bfloat16)
+        spot = jnp.where(spot, 1.0, 0.0).astype(jnp.bfloat16)
+        masks[g] = mine
+        spots[g] = spot
+        return acc + dot(mine, spot, NT)
+
+    hits = lax.fori_loop(0, 4 * groups, mark, jnp.zeros((total, TPIX), jnp.float32))
     wait_all(back_copy, total)
 
     weighted = jnp.concatenate(
@@ -477,35 +515,32 @@
         time_send[d] = stamped[:, d * N2 : (d + 1) * N2]
     start_all(time_copy, groups)
     out_ref[t] = time_send[:, pl.ds(pl.multiple_of(t * 16, 16), 16), :]
-    wait_all(time_copy, groups)
-
-    width = 8 * N2
-    own_index = lax.broadcasted_iota(jnp.int32, (total, width), 0)
-    inside_index = lax.broadcasted_iota(jnp.int32, (TPIX, width), 0)
-
-    def flat(block):
-        return jnp.concatenate([block[r : r + 1] for r in range(8)], axis=1)
-
-    def bin_rows(g, acc):
-        a = g // 4
-        b = g - a * 4
-        c = b // 2
-        rows = pl.ds(pl.multiple_of((b - c * 2) * 8, 8), 8)
-        high, low = split(flat(out_ref[a, c, rows, :]))
-        mine = jnp.broadcast_to(flat(owner_ref[a, c, rows, :]), (total, width)) == own_index
-        spot = jnp.broadcast_to(flat(inside_ref[a, c, rows, :]), (TPIX, width)) == inside_index
-        high = jnp.where(mine, jnp.broadcast_to(high.astype(jnp.float32), (total, width)), 0.0)
-        low = jnp.where(mine, jnp.broadcast_to(low.astype(jnp.float32), (total, width)), 0.0)
-        ones = jnp.where(mine, 1.0, 0.0)
-        lhs = jnp.concatenate([high, low, ones], axis=0).astype(jnp.bfloat16)
-        rhs = jnp.where(spot, 1.0, 0.0).astype(jnp.bfloat16)
-        return acc + dot(lhs, rhs, NT)
-
-    acc = lax.fori_loop(0, 4 * groups, bin_rows, jnp.zeros((3 * total, TPIX), jnp.float32))
-    acc = jnp.concatenate([acc, jnp.zeros((3 * total, 128 - TPIX), jnp.float32)], axis=1)
+
+    def bin_block(a, acc):
+        for b in range(4):
+            values = out_ref[a, b // 2, b % 2 * 8 : b % 2 * 8 + 8, :]
+            high, low = split(flat(values))
+            mine = masks[a * 4 + b]
+            lhs = jnp.concatenate(
+                [
+                    mine * jnp.broadcast_to(high, (total, width)),
+                    mine * jnp.broadcast_to(low, (total, width)),
+                ],
+                axis=0,
+            )
+            acc = acc + dot(lhs, spots[a * 4 + b], NT)
+        return acc
+
+    def bin_arrived(j, acc):
+        time_copy(j).wait()
+        return bin_block(lax.rem(t - j + groups, groups), acc)
+
+    acc = bin_block(t, jnp.zeros((2 * total, TPIX), jnp.float32))
+    acc = lax.fori_loop(1, groups, bin_arrived, acc)
+    pad = jnp.zeros((total, 128 - TPIX), jnp.float32)
     map_send[...] = jnp.zeros(map_send.shape, jnp.float32)
-    map_send[:, 0, :] = acc[:total] + acc[total : 2 * total]
-    map_send[:, 1, :] = acc[2 * total :]
+    map_send[:, 0, :] = jnp.concatenate([acc[:total] + acc[total:], pad], axis=1)
+    map_send[:, 1, :] = jnp.concatenate([hits, pad], axis=1)
     start_all(map_copy, total)
     map_recv[me] = map_send[me]
     wait_all(map_copy, total)
@@ -528,6 +563,7 @@
     pair_modes = jnp.stack([pick(modes, main_band), pick(modes, side_band)])
     pair_noise = jnp.stack([pick(noise_level, main_band), pick(noise_level, side_band)])
     pair_noise = jnp.broadcast_to(pair_noise[:, :, None], pair_modes.shape)
+    pair = jnp.concatenate([pair_modes, pair_noise], axis=2)
     everyone = det_dev * dets
     f32 = jnp.float32
     constants = [jnp.asarray(c) for c in tables()]
@@ -538,12 +574,11 @@
             jax.ShapeDtypeStruct(blocks, f32),
             jax.ShapeDtypeStruct((8, 128), f32),
         ),
-        in_specs=[vmem] * (5 + len(constants)),
+        in_specs=[vmem] * 4 + [pl.BlockSpec(memory_space=pltpu.HBM)] * len(constants),
         out_specs=(vmem, vmem),
         scratch_shapes=[
             pltpu.VMEM((2, N1, N2), f32),
-            pltpu.VMEM((2, everyone, 128), f32),
-            pltpu.VMEM((2, everyone, 128), f32),
+            pltpu.VMEM((2, everyone, 256), f32),
             pltpu.VMEM((total, 16, 128), f32),
             pltpu.VMEM((total, 16, 128), f32),
             pltpu.VMEM((total, 16, 128), f32),
@@ -552,7 +587,10 @@
             pltpu.VMEM((2, 2, everyone * 8, everyone * 8), jnp.bfloat16),
             pltpu.VMEM((total, 8, 128), f32),
             pltpu.VMEM((total, 8, 128), f32),
-            pltpu.SemaphoreType.DMA((2, dets)),
+            *[pltpu.VMEM(c.shape, c.dtype) for c in constants],
+            pltpu.VMEM((4 * groups, total, 8 * N2), jnp.bfloat16),
+            pltpu.VMEM((4 * groups, TPIX, 8 * N2), jnp.bfloat16),
+            pltpu.SemaphoreType.DMA((len(constants),)),
             pltpu.SemaphoreType.DMA((2, dets)),
             pltpu.SemaphoreType.DMA((2, groups)),
             pltpu.SemaphoreType.DMA((2, total)),
@@ -563,7 +601,7 @@
         compiler_params=pltpu.CompilerParams(
             collective_id=0, has_side_effects=True, vmem_limit_bytes=40 * 1024 * 1024
         ),
-    )(tod.reshape(blocks), owner, inside, pair_modes, pair_noise, *constants)
+    )(tod.reshape(blocks), owner, inside, pair, *constants)
     return out.reshape(tod.shape), binned[0, :TPIX]
 
 

time: 67.2 us -> 55.2 us (0.82)
  Pallas kernels: 60.8 us -> 49.4 us
    pallas_call x1, Pallas kernels: 60.8 us -> 49.4 us  [fast_body(): pl.pallas_call(functools.partial(fused, groups, dets), out_shape=(jax.Sha...]
where the time goes in v2:
time: 55.2 us; the launch traced here: 54.9 us
  Pallas kernels  49.4 us (89%)
  local copies, waits for them, and re-layouts  4.54 us (8%)
  between operations  0.76 us (1%)
    pallas_call x1, Pallas kernels, fast_body(): pl.pallas_call(functools.partial(fused, groups, dets), out_shape=(jax.Sha...  49.4 us
    unnamed x20, local copies, waits for them, and re-layouts  3.19 us

profile of v2, /device:TPU:0, one launch (start us, length us, event | category | flops | bytes accessed | tf_op | source)
XLA Modules:
  0.0 54.9 jit_solution(10509179310883591038)
XLA Ops:
  0.6 0.0 copy-start.7
  0.6 0.8 %constant_dynamic-slice_fusion.1 = (f32[1,16]{1,0:T(1,128)S(1)}, f32[1,16]{1,0:T(1,128)S(1)}) fusion(f32[4,16]{1,0:T(4,128)} %param.12, s32[]{:T(128)S(6)} %select_n.24, s32[]{:T(128)S(6)} %select_n.25), kind=kLoop, calls=%fused_computation.8 | loop fusion | bytes 264 | tf_op jit(solution)/shard_map/jit(dynamic_index_in_dim)/dynamic_slice | solution.py:76
  1.4 0.0 copy-start.6
  1.4 0.1 broadcast_in_dim.2
  1.5 0.0 copy-done.7
  1.5 0.0 copy-start.3
  1.5 1.1 %copy.12 = f32[2,8,16,256]{3,2,1,0:T(8,128)S(1)} copy(f32[2,8,16,256]{3,1,2,0:T(8,128)} %bitcast.20) | data formatting | bytes 524288
  2.6 0.0 copy-done.6
  2.6 0.0 copy-start.2
  2.7 0.0 copy-start.4
  2.7 0.0 copy-start.5
  2.7 0.3 add_select_fusion
  2.9 0.0 copy-start
  2.9 0.0 copy-start.1
  3.0 0.1 copy.14
  3.0 0.1 copy.13
  3.1 0.0 copy-done.3
  3.1 0.5 copy-done.2
  3.7 0.0 copy-done.4
  3.7 0.0 copy-done.5
  3.7 0.3 copy-done
  4.0 0.2 copy-done.1
  4.2 49.4 %shard_map.113 = (f32[8,2,16,256]{3,2,1,0:T(8,128)S(1)}, f32[8,128]{1,0:T(8,128)S(1)}) custom-call(f32[8,2,16,256]{3,2,1,0:T(8,128)S(1)} %bitcast.14, s32[8,2,16,256]{3,2,1,0:T(8,128)S(1)} %bitcast.16, s32[8,2,16,256]{3,2,1,0:T(8,128)S(1)} %bitcast.15, f32[2,16,256]{2,1,0:T(8,128)S(1)} %pad_maximum_fusion.mode_ref, bf16[2,128,128]{2,1,0:T(8,128)(2,1)S(1)} %copy-done.5, ...), custom_call_target="tpu_custom_call" | custom-call | tf_op jit(solution)/shard_map/pallas_call | solution.py:571
  53.6 0.9 %copy.15 = f32[2,8,16,256]{3,1,2,0:T(8,128)} copy(f32[2,8,16,256]{3,2,1,0:T(8,128)S(1)} %bitcast.17) | data formatting | bytes 524288
  54.4 0.5 slice_bitcast_fusion
  (3 shorter events, 0.0 us)
Async XLA Ops:
  0.6 0.9 %copy-start.7 = (f32[4,16,128]{2,1,0:T(8,128)S(1)}, f32[4,16,128]{2,1,0:T(8,128)}, u32[]{:S(2)}) copy-start(f32[4,16,128]{2,1,0:T(8,128)} %param.13) | copy-start | bytes 98308
  1.4 1.2 %copy-start.6 = (s32[16,4096]{1,0:T(8,128)S(1)}, s32[16,4096]{1,0:T(8,128)}, u32[]{:S(2)}) copy-start(s32[16,4096]{1,0:T(8,128)} %param.11) | copy-start | bytes 786436
  1.5 1.6 %copy-start.3 = (f32[4,128,256]{2,1,0:T(8,128)S(1)}, f32[4,128,256]{2,1,0:T(8,128)}, u32[]{:S(2)}) copy-start(f32[4,128,256]{2,1,0:T(8,128)} %constant.55.clone.twiddle_hbm) | copy-start | bytes 1572868
  2.6 1.1 %copy-start.2 = (bf16[2,256,512]{2,1,0:T(8,128)(2,1)S(1)}, bf16[2,256,512]{2,1,0:T(8,128)(2,1)}, u32[]{:S(2)}) copy-start(bf16[2,256,512]{2,1,0:T(8,128)(2,1)} %constant.56.clone.last_hbm) | copy-start | bytes 1572868
  2.7 1.0 %copy-start.4 = (bf16[2,128,128]{2,1,0:T(8,128)(2,1)S(1)}, bf16[2,128,128]{2,1,0:T(8,128)(2,1)}, u32[]{:S(2)}) copy-start(bf16[2,128,128]{2,1,0:T(8,128)(2,1)} %constant.59.clone.first_t_hbm) | copy-start | bytes 196612
  2.7 1.0 %copy-start.5 = (bf16[2,128,128]{2,1,0:T(8,128)(2,1)S(1)}, bf16[2,128,128]{2,1,0:T(8,128)(2,1)}, u32[]{:S(2)}) copy-start(bf16[2,128,128]{2,1,0:T(8,128)(2,1)} %constant.54.clone.first_hbm) | copy-start | bytes 196612
  2.9 1.1 %copy-start = (f32[4,256,128]{2,1,0:T(8,128)S(1)}, f32[4,256,128]{2,1,0:T(8,128)}, u32[]{:S(2)}) copy-start(f32[4,256,128]{2,1,0:T(8,128)} %constant.58.clone.twiddle_t_hbm) | copy-start | bytes 1572868
  2.9 1.2 %copy-start.1 = (bf16[2,512,256]{2,1,0:T(8,128)(2,1)S(1)}, bf16[2,512,256]{2,1,0:T(8,128)(2,1)}, u32[]{:S(2)}) copy-start(bf16[2,512,256]{2,1,0:T(8,128)(2,1)} %constant.57.clone.last_t_hbm) | copy-start | bytes 1572868

commit v3 on v2

--- a/solution.py
+++ b/solution.py
@@ -231,7 +231,7 @@
     return dot(a[0], b[0], dims) + dot(a[0], b[1], dims) + dot(a[1], b[0], dims)
 
 
-def invert_pair(matrix):
+def eliminate(matrix, begin, end):
     size, lanes = matrix.shape
     row = lax.broadcasted_iota(jnp.int32, (size, lanes), 0)
     lane = lax.broadcasted_iota(jnp.int32, (size, lanes), 1)
@@ -251,7 +251,7 @@
         base = jnp.where(at_row | at_col, 0.0, a)
         return base - jnp.where(at_row, -1.0, c) * r
 
-    return lax.fori_loop(0, size, step, matrix)
+    return lax.fori_loop(begin, end, step, matrix)
 
 
 def expand(matrix):
@@ -412,6 +412,23 @@
     x_in[:, pl.ds(pl.multiple_of(t * 16, 16), 16), :] = tod_ref[t]
     for load in loads:
         load.wait()
+    wait_all(mode_copy, dets)
+
+    count = modes_all.shape[1]
+    square = (count, count)
+    diagonal = lax.broadcasted_iota(jnp.int32, square, 0) == lax.broadcasted_iota(
+        jnp.int32, square, 1
+    )
+    sides = []
+    for s in range(2):
+        basis = modes_all[s, :, :128]
+        outer = lax.dot_general(
+            basis, basis, NT, precision=HIGHEST, preferred_element_type=jnp.float32
+        )
+        sides.append(outer + jnp.where(diagonal, modes_all[s, :, 128 : 128 + count], 0.0))
+    early = count * 3 // 8
+    partial = eliminate(jnp.concatenate(sides, axis=1), 0, early)
+
     wait_all(tod_copy, groups)
     grid = jnp.concatenate([x_in[0], x_in[1]], axis=1)
     section = dot3((first_ref[0], first_ref[1]), split(grid), NN)
@@ -436,21 +453,7 @@
         )
     start_all(spec_copy, total)
     spec_recv[me] = spec_send[chunk]
-    wait_all(mode_copy, dets)
-
-    count = modes_all.shape[1]
-    square = (count, count)
-    diagonal = lax.broadcasted_iota(jnp.int32, square, 0) == lax.broadcasted_iota(
-        jnp.int32, square, 1
-    )
-    sides = []
-    for s in range(2):
-        basis = modes_all[s, :, :128]
-        outer = lax.dot_general(
-            basis, basis, NT, precision=HIGHEST, preferred_element_type=jnp.float32
-        )
-        sides.append(outer + jnp.where(diagonal, modes_all[s, :, 128 : 128 + count], 0.0))
-    inverse = invert_pair(jnp.concatenate(sides, axis=1))
+    inverse = eliminate(partial, early, count)
     for s in range(2):
         parts = expand(inverse[:, s * count : (s + 1) * count])
         kron[s, 0] = parts[0]
@@ -585,8 +588,8 @@
             pltpu.VMEM((total, 16, 128), f32),
             pltpu.VMEM((2, N1, N2), f32),
             pltpu.VMEM((2, 2, everyone * 8, everyone * 8), jnp.bfloat16),
-            pltpu.VMEM((total, 8, 128), f32),
-            pltpu.VMEM((total, 8, 128), f32),
+            pltpu.VMEM((total, 2, 128), f32),
+            pltpu.VMEM((total, 2, 128), f32),
             *[pltpu.VMEM(c.shape, c.dtype) for c in constants],
             pltpu.VMEM((4 * groups, total, 8 * N2), jnp.bfloat16),
             pltpu.VMEM((4 * groups, TPIX, 8 * N2), jnp.bfloat16),

time: 55.2 us -> 53.7 us (0.973)
  Pallas kernels: 49.4 us -> 47.9 us
    pallas_call x1, Pallas kernels: 49.4 us -> 47.9 us  [fast_body(): pl.pallas_call(functools.partial(fused, groups, dets), out_shape=(jax.Sha...]
where the time goes in v3:
time: 53.7 us; the launch traced here: 53.5 us
  Pallas kernels  47.9 us (89%)
  local copies, waits for them, and re-layouts  4.54 us (8%)
  between operations  0.76 us (1%)
    pallas_call x1, Pallas kernels, fast_body(): pl.pallas_call(functools.partial(fused, groups, dets), out_shape=(jax.Sha...  47.9 us
    unnamed x20, local copies, waits for them, and re-layouts  3.19 us

profile of v3, /device:TPU:0, one launch (start us, length us, event | category | flops | bytes accessed | tf_op | source)
XLA Modules:
  0.0 53.5 jit_solution(1720255046734837685)
XLA Ops:
  0.6 0.0 copy-start.7
  0.6 0.8 %constant_dynamic-slice_fusion.1 = (f32[1,16]{1,0:T(1,128)S(1)}, f32[1,16]{1,0:T(1,128)S(1)}) fusion(f32[4,16]{1,0:T(4,128)} %param.12, s32[]{:T(128)S(6)} %select_n.24, s32[]{:T(128)S(6)} %select_n.25), kind=kLoop, calls=%fused_computation.8 | loop fusion | bytes 264 | tf_op jit(solution)/shard_map/jit(dynamic_index_in_dim)/dynamic_slice | solution.py:76
  1.4 0.0 copy-start.6
  1.4 0.1 broadcast_in_dim.2
  1.5 0.0 copy-done.7
  1.5 0.0 copy-start.3
  1.5 1.1 %copy.12 = f32[2,8,16,256]{3,2,1,0:T(8,128)S(1)} copy(f32[2,8,16,256]{3,1,2,0:T(8,128)} %bitcast.20) | data formatting | bytes 524288
  2.6 0.0 copy-done.6
  2.6 0.0 copy-start.2
  2.7 0.0 copy-start.4
  2.7 0.0 copy-start.5
  2.7 0.3 add_select_fusion
  2.9 0.0 copy-start
  2.9 0.0 copy-start.1
  3.0 0.1 copy.14
  3.0 0.1 copy.13
  3.1 0.0 copy-done.3
  3.1 0.5 %copy-done.2 = bf16[2,256,512]{2,1,0:T(8,128)(2,1)S(1)} copy-done((bf16[2,256,512]{2,1,0:T(8,128)(2,1)S(1)}, bf16[2,256,512]{2,1,0:T(8,128)(2,1)}, u32[]{:S(2)}) %copy-start.2) | copy-done | bytes 524312
  3.7 0.0 copy-done.4
  3.7 0.0 copy-done.5
  3.7 0.3 copy-done
  4.0 0.2 copy-done.1
  4.2 47.9 %shard_map.113 = (f32[8,2,16,256]{3,2,1,0:T(8,128)S(1)}, f32[8,128]{1,0:T(8,128)S(1)}) custom-call(f32[8,2,16,256]{3,2,1,0:T(8,128)S(1)} %bitcast.14, s32[8,2,16,256]{3,2,1,0:T(8,128)S(1)} %bitcast.16, s32[8,2,16,256]{3,2,1,0:T(8,128)S(1)} %bitcast.15, f32[2,16,256]{2,1,0:T(8,128)S(1)} %pad_maximum_fusion.mode_ref, bf16[2,128,128]{2,1,0:T(8,128)(2,1)S(1)} %copy-done.5, ...), custom_call_target="tpu_custom_call" | custom-call | tf_op jit(solution)/shard_map/pallas_call | solution.py:574
  52.1 0.9 %copy.15 = f32[2,8,16,256]{3,1,2,0:T(8,128)} copy(f32[2,8,16,256]{3,2,1,0:T(8,128)S(1)} %bitcast.17) | data formatting | bytes 524288
  53.0 0.5 slice_bitcast_fusion
  (3 shorter events, 0.0 us)
Async XLA Ops:
  0.6 0.9 %copy-start.7 = (f32[4,16,128]{2,1,0:T(8,128)S(1)}, f32[4,16,128]{2,1,0:T(8,128)}, u32[]{:S(2)}) copy-start(f32[4,16,128]{2,1,0:T(8,128)} %param.13) | copy-start | bytes 98308
  1.4 1.2 %copy-start.6 = (s32[16,4096]{1,0:T(8,128)S(1)}, s32[16,4096]{1,0:T(8,128)}, u32[]{:S(2)}) copy-start(s32[16,4096]{1,0:T(8,128)} %param.11) | copy-start | bytes 786436
  1.5 1.6 %copy-start.3 = (f32[4,128,256]{2,1,0:T(8,128)S(1)}, f32[4,128,256]{2,1,0:T(8,128)}, u32[]{:S(2)}) copy-start(f32[4,128,256]{2,1,0:T(8,128)} %constant.55.clone.twiddle_hbm) | copy-start | bytes 1572868
  2.6 1.1 %copy-start.2 = (bf16[2,256,512]{2,1,0:T(8,128)(2,1)S(1)}, bf16[2,256,512]{2,1,0:T(8,128)(2,1)}, u32[]{:S(2)}) copy-start(bf16[2,256,512]{2,1,0:T(8,128)(2,1)} %constant.56.clone.last_hbm) | copy-start | bytes 1572868
  2.7 1.0 %copy-start.4 = (bf16[2,128,128]{2,1,0:T(8,128)(2,1)S(1)}, bf16[2,128,128]{2,1,0:T(8,128)(2,1)}, u32[]{:S(2)}) copy-start(bf16[2,128,128]{2,1,0:T(8,128)(2,1)} %constant.59.clone.first_t_hbm) | copy-start | bytes 196612
  2.7 1.0 %copy-start.5 = (bf16[2,128,128]{2,1,0:T(8,128)(2,1)S(1)}, bf16[2,128,128]{2,1,0:T(8,128)(2,1)}, u32[]{:S(2)}) copy-start(bf16[2,128,128]{2,1,0:T(8,128)(2,1)} %constant.54.clone.first_hbm) | copy-start | bytes 196612
  2.9 1.1 %copy-start = (f32[4,256,128]{2,1,0:T(8,128)S(1)}, f32[4,256,128]{2,1,0:T(8,128)}, u32[]{:S(2)}) copy-start(f32[4,256,128]{2,1,0:T(8,128)} %constant.58.clone.twiddle_t_hbm) | copy-start | bytes 1572868
  2.9 1.2 %copy-start.1 = (bf16[2,512,256]{2,1,0:T(8,128)(2,1)S(1)}, bf16[2,512,256]{2,1,0:T(8,128)(2,1)}, u32[]{:S(2)}) copy-start(bf16[2,512,256]{2,1,0:T(8,128)(2,1)} %constant.57.clone.last_t_hbm) | copy-start | bytes 1572868

commit v4 on v3

--- a/solution.py
+++ b/solution.py
@@ -171,7 +171,7 @@
 N1 = 128
 N2 = 256
 CHUNKS = 32
-UNROLL = 1
+UNROLL = True
 MESH = pl.DeviceIdType.MESH
 NT = (((1,), (1,)), ((), ()))
 NN = (((1,), (0,)), ((), ()))

time: 53.7 us -> 53.6 us (level)
  no operation moved by 1% of the time
where the time goes in v4:
time: 53.6 us; the launch traced here: 53.4 us
  Pallas kernels  47.8 us (89%)
  local copies, waits for them, and re-layouts  4.54 us (8%)
  between operations  0.76 us (1%)
    pallas_call x1, Pallas kernels, fast_body(): pl.pallas_call(functools.partial(fused, groups, dets), out_shape=(jax.Sha...  47.8 us
    unnamed x20, local copies, waits for them, and re-layouts  3.19 us

profile of v4, /device:TPU:0, one launch (start us, length us, event | category | flops | bytes accessed | tf_op | source)
XLA Modules:
  0.0 53.4 jit_solution(1021730058200118912)
XLA Ops:
  0.6 0.0 copy-start.7
  0.6 0.8 %constant_dynamic-slice_fusion.1 = (f32[1,16]{1,0:T(1,128)S(1)}, f32[1,16]{1,0:T(1,128)S(1)}) fusion(f32[4,16]{1,0:T(4,128)} %param.12, s32[]{:T(128)S(6)} %select_n.24, s32[]{:T(128)S(6)} %select_n.25), kind=kLoop, calls=%fused_computation.8 | loop fusion | bytes 264 | tf_op jit(solution)/shard_map/jit(dynamic_index_in_dim)/dynamic_slice | solution.py:76
  1.4 0.0 copy-start.6
  1.4 0.1 broadcast_in_dim.2
  1.5 0.0 copy-done.7
  1.5 0.0 copy-start.3
  1.5 1.1 %copy.12 = f32[2,8,16,256]{3,2,1,0:T(8,128)S(1)} copy(f32[2,8,16,256]{3,1,2,0:T(8,128)} %bitcast.20) | data formatting | bytes 524288
  2.6 0.0 copy-done.6
  2.6 0.0 copy-start.2
  2.7 0.0 copy-start.4
  2.7 0.0 copy-start.5
  2.7 0.3 add_select_fusion
  2.9 0.0 copy-start
  2.9 0.0 copy-start.1
  3.0 0.1 copy.14
  3.0 0.1 copy.13
  3.1 0.0 copy-done.3
  3.1 0.5 %copy-done.2 = bf16[2,256,512]{2,1,0:T(8,128)(2,1)S(1)} copy-done((bf16[2,256,512]{2,1,0:T(8,128)(2,1)S(1)}, bf16[2,256,512]{2,1,0:T(8,128)(2,1)}, u32[]{:S(2)}) %copy-start.2) | copy-done | bytes 524312
  3.7 0.0 copy-done.4
  3.7 0.0 copy-done.5
  3.7 0.3 copy-done
  4.0 0.2 copy-done.1
  4.2 47.8 %shard_map.113 = (f32[8,2,16,256]{3,2,1,0:T(8,128)S(1)}, f32[8,128]{1,0:T(8,128)S(1)}) custom-call(f32[8,2,16,256]{3,2,1,0:T(8,128)S(1)} %bitcast.14, s32[8,2,16,256]{3,2,1,0:T(8,128)S(1)} %bitcast.16, s32[8,2,16,256]{3,2,1,0:T(8,128)S(1)} %bitcast.15, f32[2,16,256]{2,1,0:T(8,128)S(1)} %pad_maximum_fusion.mode_ref, bf16[2,128,128]{2,1,0:T(8,128)(2,1)S(1)} %copy-done.5, ...), custom_call_target="tpu_custom_call" | custom-call | tf_op jit(solution)/shard_map/pallas_call | solution.py:574
  52.0 0.9 %copy.15 = f32[2,8,16,256]{3,1,2,0:T(8,128)} copy(f32[2,8,16,256]{3,2,1,0:T(8,128)S(1)} %bitcast.17) | data formatting | bytes 524288
  52.9 0.5 slice_bitcast_fusion
  (3 shorter events, 0.0 us)
Async XLA Ops:
  0.6 0.9 %copy-start.7 = (f32[4,16,128]{2,1,0:T(8,128)S(1)}, f32[4,16,128]{2,1,0:T(8,128)}, u32[]{:S(2)}) copy-start(f32[4,16,128]{2,1,0:T(8,128)} %param.13) | copy-start | bytes 98308
  1.4 1.2 %copy-start.6 = (s32[16,4096]{1,0:T(8,128)S(1)}, s32[16,4096]{1,0:T(8,128)}, u32[]{:S(2)}) copy-start(s32[16,4096]{1,0:T(8,128)} %param.11) | copy-start | bytes 786436
  1.5 1.6 %copy-start.3 = (f32[4,128,256]{2,1,0:T(8,128)S(1)}, f32[4,128,256]{2,1,0:T(8,128)}, u32[]{:S(2)}) copy-start(f32[4,128,256]{2,1,0:T(8,128)} %constant.55.clone.twiddle_hbm) | copy-start | bytes 1572868
  2.6 1.1 %copy-start.2 = (bf16[2,256,512]{2,1,0:T(8,128)(2,1)S(1)}, bf16[2,256,512]{2,1,0:T(8,128)(2,1)}, u32[]{:S(2)}) copy-start(bf16[2,256,512]{2,1,0:T(8,128)(2,1)} %constant.56.clone.last_hbm) | copy-start | bytes 1572868
  2.7 1.0 %copy-start.4 = (bf16[2,128,128]{2,1,0:T(8,128)(2,1)S(1)}, bf16[2,128,128]{2,1,0:T(8,128)(2,1)}, u32[]{:S(2)}) copy-start(bf16[2,128,128]{2,1,0:T(8,128)(2,1)} %constant.59.clone.first_t_hbm) | copy-start | bytes 196612
  2.7 1.0 %copy-start.5 = (bf16[2,128,128]{2,1,0:T(8,128)(2,1)S(1)}, bf16[2,128,128]{2,1,0:T(8,128)(2,1)}, u32[]{:S(2)}) copy-start(bf16[2,128,128]{2,1,0:T(8,128)(2,1)} %constant.54.clone.first_hbm) | copy-start | bytes 196612
  2.9 1.1 %copy-start = (f32[4,256,128]{2,1,0:T(8,128)S(1)}, f32[4,256,128]{2,1,0:T(8,128)}, u32[]{:S(2)}) copy-start(f32[4,256,128]{2,1,0:T(8,128)} %constant.58.clone.twiddle_t_hbm) | copy-start | bytes 1572868
  2.9 1.2 %copy-start.1 = (bf16[2,512,256]{2,1,0:T(8,128)(2,1)S(1)}, bf16[2,512,256]{2,1,0:T(8,128)(2,1)}, u32[]{:S(2)}) copy-start(bf16[2,512,256]{2,1,0:T(8,128)(2,1)} %constant.57.clone.last_t_hbm) | copy-start | bytes 1572868
